TPU v7x, 128 devices: a whole 4x4x4 slice. The times are simulated.
128 devices in a mesh: spec: 16 (over y_lo, x, core), wave: 8 (over z, y_hi).
Axes of the slice: x: 4, y: 4 (y_hi: 2, y_lo: 2; y = y_hi * 2 + y_lo), z: 4, core: 2. Of those that a mesh axis runs over, the one named last changes fastest.
Arguments:
- spectra: bfloat16 [16384, 7168], P('spec', 'wave'), may hold values from 0.049804688 to 5
- offsets: int32 [64], P('spec'), may hold values from 0 to 7167, as said below
- cover_lo: int32 [16384], P('spec'), may hold values from 0 to 7167, as said below
- cover_hi: int32 [16384], P('spec'), may hold values from 5377 to 7168
- coefficients: float32 [16384, 128], P('spec'), may hold values from 0.03 to 0.3
- templates: float32 [128, 7168], P(None, 'wave'), may hold values from 0.03 to 0.3
Outputs:
- templates_new: float32 [128, 7168], P(None, 'wave')
- coefficients_new: float32 [16384, 128], P('spec')
Inputs may be any that keep to these rules, and one draw needn't show every extreme that they name: `offsets`: the first block of each index of spec has an offset of at least 6272; the last block's offset is 7167. cover_lo < cover_hi for every spectrum; about one spectrum in eight has weight one only on its last 1 to 4 observed pixels, cover_hi = 7168; the others have cover_lo < 1792 and cover_hi > 5376.
All inputs are finite; a program needn't handle non-finite values.
Results may differ from a plain program's by a relative error of at most 0.0012.
Values may be sent and summed in bfloat16 or wider, within the bound.
No kernel may reach another device: no remote copies, remote signals or barrier semaphores. Data moves between devices by JAX's collectives and lax.ppermute only.
A program may use at most 128 MiB of HBM per device.

v0:
```python
import jax
import jax.numpy as jnp
from jax import lax
from jax.sharding import PartitionSpec as P

ITERS = 4


def take_blocks(joined, starts, blocks, width):
    rows = joined.shape[0]
    grouped = joined.reshape(blocks, rows // blocks, joined.shape[1])
    picked = jax.vmap(lambda piece, start: lax.dynamic_slice_in_dim(piece, start, width, 1))(
        grouped, starts
    )
    return picked.reshape(rows, width)


def ratio_of(rest, weight, coef_bf, temps_bf):
    model = jnp.dot(coef_bf, temps_bf, preferred_element_type=jnp.float32)
    inside = weight > 0
    return jnp.where(inside, rest.astype(jnp.float32) / jnp.where(inside, model, 1.0), 0.0).astype(
        jnp.bfloat16
    )


def over_rows(left, right):
    return lax.dot_general(
        left, right, (((0,), (0,)), ((), ())), preferred_element_type=jnp.float32
    )


def over_pixels(left, right):
    return lax.dot_general(
        left, right, (((1,), (1,)), ((), ())), preferred_element_type=jnp.float32
    )


def template_update(temps, num_t, den_t):
    num_a, den_a = lax.psum((num_t, den_t), "spec")
    return temps * num_a / jnp.maximum(den_a, 1.0)


def coef_update(coef, num_c, den_c):
    num_a, den_a = lax.psum((num_c, den_c), "wave")
    return coef * num_a / jnp.maximum(den_a, 1.0)


def shards(spectra, offsets, cover_lo, cover_hi, coefficients, templates):
    rows, width = spectra.shape
    blocks = offsets.shape[0]
    block_rows = rows // blocks
    wave_pos = lax.axis_index("wave")
    row_off = jnp.repeat(offsets, block_rows)
    whole = lax.all_gather(spectra, "wave", axis=1, tiled=True)
    joined = jnp.concatenate([whole, jnp.zeros((rows, width), whole.dtype)], axis=1)
    starts = jnp.minimum(wave_pos * width + offsets, whole.shape[1])
    rest = take_blocks(joined, starts, blocks, width)
    pixel = wave_pos * width + jnp.arange(width, dtype=jnp.int32)
    observed = pixel[None, :] + row_off[:, None]
    weight = ((observed >= cover_lo[:, None]) & (observed < cover_hi[:, None])).astype(jnp.bfloat16)
    temps = templates
    coef = coefficients
    for update in range(ITERS):
        coef_bf = coef.astype(jnp.bfloat16)
        ratio = ratio_of(rest, weight, coef_bf, temps.astype(jnp.bfloat16))
        temps = template_update(temps, over_rows(coef_bf, ratio), over_rows(coef_bf, weight))
        temps_bf = temps.astype(jnp.bfloat16)
        ratio_new = ratio_of(rest, weight, coef_bf, temps_bf)
        coef = coef_update(coef, over_pixels(ratio_new, temps_bf), over_pixels(weight, temps_bf))
    return (temps, coef)


def solution(mesh):
    in_specs = (
        P("spec", "wave"),
        P("spec"),
        P("spec"),
        P("spec"),
        P("spec", None),
        P(None, "wave"),
    )
    out_specs = (P(None, "wave"), P("spec", None))
    return jax.shard_map(shards, mesh=mesh, in_specs=in_specs, out_specs=out_specs, check_vma=False)
```

profile of v0, /device:TPU:0, one launch (start us, length us, event | category | flops | bytes accessed | tf_op | source)
XLA Modules:
  0.0 1094.5 jit_solution(7808599163899580070)
XLA Ops:
  7.2 0.0 all-gather.2.cloned.1.call-start
  7.2 0.7 all-gather.2.cloned.1.call-update
  7.9 0.0 all-reduce.25.cloned.1.call-start
  8.0 0.7 broadcast_bitcast_fusion
  8.7 0.7 fusion.32
  9.4 0.1 copy.8
  9.5 3.4 convolution_bitcast_fusion
  12.9 163.0 %all-gather.2.cloned.1.call-done = bf16[1024,7168]{1,0:T(8,128)(2,1)} async-done(((bf16[1024,896]{1,0:T(8,128)(2,1)}), bf16[1024,7168]{1,0:T(8,128)(2,1)}) %all-gather.2.cloned.1.call-update) | async-done | bytes 14680080 | tf_op jit(solution)/shard_map/all_gather | solution.py:54
  175.9 12.9 %concatenate.6 = bf16[1024,8064]{1,0:T(8,128)(2,1)} pad(bf16[1024,7168]{1,0:T(8,128)(2,1)} %all-gather.2.cloned.1.call-done, bf16[]{:T(256)} %constant.10.clone.1), padding=0_0x0_896 | pad | bytes 31195138 | tf_op jit(solution)/shard_map/concatenate | solution.py:55
  188.8 12.5 %while.1 = (s32[]{:T(128)}, bf16[4,256,8064]{2,1,0:T(8,128)(2,1)}, s32[4,3]{1,0:T(4,128)S(1)}, bf16[4,256,896]{2,1,0:T(8,128)(2,1)S(1)}, s32[]{:T(128)}) while((s32[]{:T(128)}, bf16[4,256,8064]{2,1,0:T(8,128)(2,1)}, s32[4,3]{1,0:T(4,128)S(1)}, bf16[4,256,896]{2,1,0:T(8,128)(2,1)S(1)}, s32[]{:T(128)}) %tuple.54), condition=%wide.while_cond, body=%wide.while_body.sunk | while | flops 2 | bytes 917621 | solution.py:12
  188.8 0.6 fusion.108
  189.4 2.5 dynamic-slice_dynamic-update-slice_fusion.2
  191.9 0.6 fusion.108
  192.5 2.5 dynamic-slice_dynamic-update-slice_fusion.2
  195.1 0.6 fusion.108
  195.7 2.5 dynamic-slice_dynamic-update-slice_fusion.2
  198.2 0.6 fusion.108
  198.8 2.5 dynamic-slice_dynamic-update-slice_fusion.2
  201.4 2.9 fusion.25
  204.3 0.0 all-reduce.25.cloned.1.call-update
  204.3 0.0 all-reduce.33.cloned.1.call-start
  204.3 0.2 copy.9
  204.5 116.8 %all-reduce.25.cloned.1.call-done = (f32[128,896]{0,1:T(8,128)}, f32[128,896]{0,1:T(8,128)}) async-done(((f32[128,896]{0,1:T(8,128)}, f32[128,896]{0,1:T(8,128)}), (f32[128,896]{0,1:T(8,128)}, f32[128,896]{0,1:T(8,128)})) %all-reduce.25.cloned.1.call-update) | async-done | bytes 917520 | tf_op jit(solution)/shard_map/psum | solution.py:39
  321.3 1.2 maximum_divide_fusion.7
  322.6 2.5 fusion.20
  325.1 2.0 fusion.63
  327.0 0.0 all-reduce.33.cloned.1.call-update
  327.1 0.0 all-reduce.23.cloned.1.call-start
  327.1 92.3 %all-reduce.33.cloned.1.call-done = (f32[1024,128]{1,0:T(8,128)}, f32[1024,128]{1,0:T(8,128)}) async-done(((f32[1024,128]{1,0:T(8,128)}, f32[1024,128]{1,0:T(8,128)}), (f32[1024,128]{1,0:T(8,128)}, f32[1024,128]{1,0:T(8,128)})) %all-reduce.33.cloned.1.call-update) | async-done | bytes 1048592 | tf_op jit(solution)/shard_map/psum | solution.py:44
  419.4 1.3 maximum_divide_fusion.3
  420.7 3.2 fusion.24
  423.9 2.4 fusion.57
  426.3 0.0 all-reduce.23.cloned.1.call-update
  426.3 0.2 all-reduce.31.cloned.1.call-start
  426.5 117.0 %all-reduce.23.cloned.1.call-done = (f32[128,896]{0,1:T(8,128)}, f32[128,896]{0,1:T(8,128)}) async-done(((f32[128,896]{0,1:T(8,128)}, f32[128,896]{0,1:T(8,128)}), (f32[128,896]{0,1:T(8,128)}, f32[128,896]{0,1:T(8,128)})) %all-reduce.23.cloned.1.call-update) | async-done | bytes 917520 | tf_op jit(solution)/shard_map/psum | solution.py:39
  543.5 1.2 maximum_divide_fusion.6
  544.7 2.5 fusion.19
  547.3 2.0 fusion.51
  549.2 0.0 all-reduce.21.cloned.1.call-start
  549.3 92.2 %all-reduce.31.cloned.1.call-done = (f32[1024,128]{1,0:T(8,128)}, f32[1024,128]{1,0:T(8,128)}) async-done(((f32[1024,128]{1,0:T(8,128)}, f32[1024,128]{1,0:T(8,128)}), (f32[1024,128]{1,0:T(8,128)}, f32[1024,128]{1,0:T(8,128)})) %all-reduce.31.cloned.1.call-update) | async-done | bytes 1048592 | tf_op jit(solution)/shard_map/psum | solution.py:44
  641.5 1.3 maximum_divide_fusion.2
  642.8 3.2 fusion.23
  646.0 2.4 fusion.45
  648.4 0.0 all-reduce.21.cloned.1.call-update
  648.4 0.0 all-reduce.29.cloned.1.call-start
  648.5 117.2 %all-reduce.21.cloned.1.call-done = (f32[128,896]{0,1:T(8,128)}, f32[128,896]{0,1:T(8,128)}) async-done(((f32[128,896]{0,1:T(8,128)}, f32[128,896]{0,1:T(8,128)}), (f32[128,896]{0,1:T(8,128)}, f32[128,896]{0,1:T(8,128)})) %all-reduce.21.cloned.1.call-update) | async-done | bytes 917520 | tf_op jit(solution)/shard_map/psum | solution.py:39
  765.6 1.2 maximum_divide_fusion.5
  766.8 2.5 fusion.18
  769.4 2.0 fusion.39
  771.3 0.0 all-reduce.29.cloned.1.call-update
  771.4 0.3 all-reduce.19.cloned.1.call-start
  771.6 92.1 %all-reduce.29.cloned.1.call-done = (f32[1024,128]{1,0:T(8,128)}, f32[1024,128]{1,0:T(8,128)}) async-done(((f32[1024,128]{1,0:T(8,128)}, f32[1024,128]{1,0:T(8,128)}), (f32[1024,128]{1,0:T(8,128)}, f32[1024,128]{1,0:T(8,128)})) %all-reduce.29.cloned.1.call-update) | async-done | bytes 1048592 | tf_op jit(solution)/shard_map/psum | solution.py:44
  863.7 1.3 maximum_divide_fusion.1
  865.0 3.2 fusion.22
  868.2 2.4 fusion.33
  870.5 0.0 all-reduce.19.cloned.1.call-update
  870.6 0.0 all-reduce.27.cloned.1.call-start
  870.6 117.2 %all-reduce.19.cloned.1.call-done = (f32[128,896]{0,1:T(8,128)}, f32[128,896]{0,1:T(8,128)}) async-done(((f32[128,896]{0,1:T(8,128)}, f32[128,896]{0,1:T(8,128)}), (f32[128,896]{0,1:T(8,128)}, f32[128,896]{0,1:T(8,128)})) %all-reduce.19.cloned.1.call-update) | async-done | bytes 917520 | tf_op jit(solution)/shard_map/psum | solution.py:39
  987.8 1.2 maximum_divide_fusion.4
  989.0 2.5 fusion.17
  991.6 2.0 fusion.30
  993.5 1.0 copy.16
  994.5 91.4 %all-reduce.27.cloned.1.call-done = (f32[1024,128]{1,0:T(8,128)}, f32[1024,128]{1,0:T(8,128)}) async-done(((f32[1024,128]{1,0:T(8,128)}, f32[1024,128]{1,0:T(8,128)}), (f32[1024,128]{1,0:T(8,128)}, f32[1024,128]{1,0:T(8,128)})) %all-reduce.27.cloned.1.call-update) | async-done | bytes 1048592 | tf_op jit(solution)/shard_map/psum | solution.py:44
  1085.9 2.1 maximum_divide_fusion
  (19 shorter events, 0.1 us)
Async XLA Ops:
  7.2 168.7 %all-gather.2.cloned.1.call-start = ((), (), s32[]{:S(2)}) async-start(), calls=%async_computation | async-start | bytes 16515072 | tf_op jit(solution)/shard_map/all_gather | solution.py:54
  7.9 313.4 %all-reduce.25.cloned.1.call-start = ((), (), s32[]{:S(2)}) async-start(), calls=%async_computation.4 | async-start | bytes 1835008 | tf_op jit(solution)/shard_map/psum | solution.py:39
  175.9 25.5 %copy-start.1 = (f32[128,896]{1,0:T(8,128)S(1)}, f32[128,896]{1,0:T(8,128)}, u32[]{:S(2)}) copy-start(f32[128,896]{1,0:T(8,128)} %param.11) | copy-start | bytes 1376260
  188.8 12.6 %copy-start = (f32[1024,128]{1,0:T(8,128)S(1)}, f32[1024,128]{1,0:T(8,128)}, u32[]{:S(2)}) copy-start(f32[1024,128]{1,0:T(8,128)} %param.10) | copy-start | bytes 1572868
  188.8 12.6 %copy-start.2 = (s32[1024]{0:T(1024)S(1)}, s32[1024]{0:T(1024)}, u32[]{:S(2)}) copy-start(s32[1024]{0:T(1024)} %param.9) | copy-start | bytes 12292
  188.8 12.6 %copy-start.3 = (s32[1024]{0:T(1024)S(1)}, s32[1024]{0:T(1024)}, u32[]{:S(2)}) copy-start(s32[1024]{0:T(1024)} %param.8) | copy-start | bytes 12292
  204.3 215.1 %all-reduce.33.cloned.1.call-start = ((), (), s32[]{:S(2)}) async-start(), calls=%async_computation.8 | async-start | bytes 2097152 | tf_op jit(solution)/shard_map/psum | solution.py:44
  327.1 216.4 %all-reduce.23.cloned.1.call-start = ((), (), s32[]{:S(2)}) async-start(), calls=%async_computation.3 | async-start | bytes 1835008 | tf_op jit(solution)/shard_map/psum | solution.py:39
  426.3 215.2 %all-reduce.31.cloned.1.call-start = ((), (), s32[]{:S(2)}) async-start(), calls=%async_computation.7 | async-start | bytes 2097152 | tf_op jit(solution)/shard_map/psum | solution.py:44
  549.2 216.4 %all-reduce.21.cloned.1.call-start = ((), (), s32[]{:S(2)}) async-start(), calls=%async_computation.2 | async-start | bytes 1835008 | tf_op jit(solution)/shard_map/psum | solution.py:39
  648.4 215.3 %all-reduce.29.cloned.1.call-start = ((), (), s32[]{:S(2)}) async-start(), calls=%async_computation.6 | async-start | bytes 2097152 | tf_op jit(solution)/shard_map/psum | solution.py:44
  771.4 216.4 %all-reduce.19.cloned.1.call-start = ((), (), s32[]{:S(2)}) async-start(), calls=%async_computation.1 | async-start | bytes 1835008 | tf_op jit(solution)/shard_map/psum | solution.py:39
  870.6 215.3 %all-reduce.27.cloned.1.call-start = ((), (), s32[]{:S(2)}) async-start(), calls=%async_computation.5 | async-start | bytes 2097152 | tf_op jit(solution)/shard_map/psum | solution.py:44
Sparse Core Ops, SparseCore 0:
  10.4 165.4 all-gather.1
  204.4 116.8 all-reduce.24
  327.2 92.1 all-reduce.32
  426.4 117.0 all-reduce.22
  549.4 92.1 all-reduce.30
  648.5 117.0 all-reduce.20
  771.5 92.1 all-reduce.28
  870.7 117.0 all-reduce.18
  993.7 92.1 all-reduce.26
where the time goes:
time: 1100 us; the launch traced here: 1090 us
  waiting for transfers between devices  1000 us (91%)
  matrix products  41 us (4%)
  local copies, waits for them, and re-layouts  27.3 us (2%)
  between operations  13.9 us (1%)
  other arithmetic  11.5 us (1%)
    psum x4, waiting for transfers between devices, template_update(): num_a, den_a = lax.psum((num_t, den_t), 'spec')  468 us
    psum x4, waiting for transfers between devices, coef_update(): num_a, den_a = lax.psum((num_c, den_c), 'wave')  368 us
    all_gather x1, waiting for transfers between devices, shards(): whole = lax.all_gather(spectra, 'wave', axis=1, tiled=True)  163 us
    dot_general x8, matrix products, over_rows(): lax.dot_general(left, right, (((0,), (0,)), ((), ())), preferred_element_...  23.1 us
  transfers between devices with their start and end apart: 9, of which 9 were waited for; matrix products, arithmetic and copies ran while one was open for 1% of the time, Pallas kernels for 0%

commit v1 on v0

--- a/solution.py
+++ b/solution.py
@@ -51,7 +51,10 @@
     block_rows = rows // blocks
     wave_pos = lax.axis_index("wave")
     row_off = jnp.repeat(offsets, block_rows)
-    whole = lax.all_gather(spectra, "wave", axis=1, tiled=True)
+    size = lax.axis_size("wave")
+    tiles = jnp.stack([spectra for _ in range(size)])
+    tiles = lax.all_to_all(tiles, "wave", split_axis=0, concat_axis=0)
+    whole = jnp.concatenate(tiles, axis=1)
     joined = jnp.concatenate([whole, jnp.zeros((rows, width), whole.dtype)], axis=1)
     starts = jnp.minimum(wave_pos * width + offsets, whole.shape[1])
     rest = take_blocks(joined, starts, blocks, width)

time: 1100 us -> 1160 us (1.055)
  local copies, waits for them, and re-layouts: 27.3 us -> 75.4 us
    all_gather x1 -> x0, waiting for transfers between devices: 163 us -> none  [shards(): whole = lax.all_gather(spectra, 'wave', axis=1, tiled=True)]
    all_to_all x0 -> x1, waiting for transfers between devices: none -> 161 us  [shards(): tiles = lax.all_to_all(tiles, 'wave', split_axis=0, concat_axis=0)]
    all_to_all x0 -> x1, local copies, waits for them, and re-layouts: none -> 20.7 us  [shards(): tiles = lax.all_to_all(tiles, 'wave', split_axis=0, concat_axis=0)]
    unnamed x14 -> x17, local copies, waits for them, and re-layouts: 2 us -> 19.9 us
  transfers between devices with their start and end apart: 9 -> 9, of which waited for: 9 -> 9; matrix products, arithmetic and copies ran while one was open for 1% -> 0% of each run, Pallas kernels for 0% -> 0%
where the time goes in v1:
time: 1160 us
  waiting for transfers between devices  996 us (86%)
  local copies, waits for them, and re-layouts  75.4 us (7%)
  matrix products  51.2 us (4%)
  between operations  14.2 us (1%)
    psum x4, waiting for transfers between devices, template_update(): num_a, den_a = lax.psum((num_t, den_t), 'spec')  468 us
    psum x4, waiting for transfers between devices, coef_update(): num_a, den_a = lax.psum((num_c, den_c), 'wave')  368 us
    all_to_all x1, waiting for transfers between devices, shards(): tiles = lax.all_to_all(tiles, 'wave', split_axis=0, concat_axis=0)  161 us
    dot_general x8, matrix products, over_rows(): lax.dot_general(left, right, (((0,), (0,)), ((), ())), preferred_element_...  27.5 us
    dot_general x8, matrix products, over_pixels(): lax.dot_general(left, right, (((1,), (1,)), ((), ())), preferred_element_...  23.7 us
  transfers between devices with their start and end apart: 9, of which 9 were waited for; matrix products, arithmetic and copies ran while one was open for 0% of the time, Pallas kernels for 0%

profile of v1, /device:TPU:0, one launch (start us, length us, event | category | flops | bytes accessed | tf_op | source)
XLA Modules:
  0.0 1156.9 jit_solution(5466918554296726977)
XLA Ops:
  7.2 6.5 stack.2
  13.7 8.2 all-to-all-start
  21.9 0.0 all-reduce.25.cloned.1.call-start
  21.9 0.1 broadcast_bitcast_fusion
  22.0 0.1 copy.28
  22.1 2.4 convolution_bitcast_fusion
  24.5 160.8 %all-to-all-done = bf16[8,1024,896]{2,1,0:T(8,128)(2,1)} async-done(((bf16[8,1024,896]{2,1,0:T(8,128)(2,1)}), bf16[8,1024,896]{2,1,0:T(8,128)(2,1)}, u32[]{:S(2)}, u32[]{:S(2)}) %all-to-all-start) | async-done | bytes 14680096 | tf_op jit(solution)/shard_map/all_to_all | solution.py:56
  185.3 20.7 %copy.26 = bf16[8,1024,896]{1,2,0:T(8,128)(2,1)} copy(bf16[8,1024,896]{2,1,0:T(8,128)(2,1)} %all-to-all-done) | data formatting | bytes 29360128 | tf_op jit(solution)/shard_map/all_to_all | solution.py:56
  205.9 18.5 %copy.46 = bf16[1024,7168]{1,0:T(8,128)(2,1)} copy(bf16[1024,7168]{0,1:T(8,128)(2,1)} %bitcast.27) | data formatting | bytes 29360128
  224.5 12.8 %concatenate.6.clone = bf16[1024,8064]{1,0:T(8,128)(2,1)} pad(bf16[1024,7168]{1,0:T(8,128)(2,1)} %copy.46, bf16[]{:T(256)} %constant.10.clone.1), padding=0_0x0_896 | pad | bytes 31195138 | tf_op jit(solution)/shard_map/concatenate | solution.py:58
  237.3 15.5 %while.1 = (s32[]{:T(128)}, bf16[4,256,8064]{2,1,0:T(8,128)(2,1)}, s32[4,3]{1,0:T(4,128)S(1)}, bf16[4,256,896]{2,1,0:T(8,128)(2,1)}, s32[]{:T(128)}) while((s32[]{:T(128)}, bf16[4,256,8064]{2,1,0:T(8,128)(2,1)}, s32[4,3]{1,0:T(4,128)S(1)}, bf16[4,256,896]{2,1,0:T(8,128)(2,1)}, s32[]{:T(128)}) %tuple.56), condition=%wide.while_cond, body=%wide.while_body.sunk | while | flops 2 | bytes 919145 | solution.py:12
  237.3 0.6 fusion.108
  237.9 3.3 dynamic-slice_dynamic-update-slice_fusion.2
  241.2 0.6 fusion.108
  241.8 3.3 dynamic-slice_dynamic-update-slice_fusion.2
  245.1 0.6 fusion.108
  245.7 3.3 dynamic-slice_dynamic-update-slice_fusion.2
  248.9 0.6 fusion.108
  249.5 3.3 dynamic-slice_dynamic-update-slice_fusion.2
  252.8 4.2 fusion.25
  257.1 0.0 all-reduce.33.cloned.1.call-start
  257.1 0.2 copy.29
  257.3 116.4 %all-reduce.25.cloned.1.call-done = (f32[128,896]{0,1:T(8,128)}, f32[128,896]{0,1:T(8,128)}) async-done(((f32[128,896]{0,1:T(8,128)}, f32[128,896]{0,1:T(8,128)}), (f32[128,896]{0,1:T(8,128)}, f32[128,896]{0,1:T(8,128)})) %all-reduce.25.cloned.1.call-update) | async-done | bytes 917520 | tf_op jit(solution)/shard_map/psum | solution.py:39
  373.7 1.2 maximum_divide_fusion.7
  374.9 4.0 fusion.20
  378.9 2.0 fusion.63
  380.8 0.0 all-reduce.33.cloned.1.call-update
  380.9 0.2 all-reduce.23.cloned.1.call-start
  381.1 92.0 %all-reduce.33.cloned.1.call-done = (f32[1024,128]{1,0:T(8,128)}, f32[1024,128]{1,0:T(8,128)}) async-done(((f32[1024,128]{1,0:T(8,128)}, f32[1024,128]{1,0:T(8,128)}), (f32[1024,128]{1,0:T(8,128)}, f32[1024,128]{1,0:T(8,128)})) %all-reduce.33.cloned.1.call-update) | async-done | bytes 1048592 | tf_op jit(solution)/shard_map/psum | solution.py:44
  473.1 1.3 maximum_divide_fusion.3
  474.4 4.6 fusion.24
  479.0 2.4 fusion.57
  481.4 0.0 all-reduce.23.cloned.1.call-update
  481.4 0.0 all-reduce.31.cloned.1.call-start
  481.4 117.2 %all-reduce.23.cloned.1.call-done = (f32[128,896]{0,1:T(8,128)}, f32[128,896]{0,1:T(8,128)}) async-done(((f32[128,896]{0,1:T(8,128)}, f32[128,896]{0,1:T(8,128)}), (f32[128,896]{0,1:T(8,128)}, f32[128,896]{0,1:T(8,128)})) %all-reduce.23.cloned.1.call-update) | async-done | bytes 917520 | tf_op jit(solution)/shard_map/psum | solution.py:39
  598.6 1.2 maximum_divide_fusion.6
  599.8 4.0 fusion.19
  603.8 2.0 fusion.51
  605.8 0.0 all-reduce.31.cloned.1.call-update
  605.8 0.0 all-reduce.21.cloned.1.call-start
  605.8 92.3 %all-reduce.31.cloned.1.call-done = (f32[1024,128]{1,0:T(8,128)}, f32[1024,128]{1,0:T(8,128)}) async-done(((f32[1024,128]{1,0:T(8,128)}, f32[1024,128]{1,0:T(8,128)}), (f32[1024,128]{1,0:T(8,128)}, f32[1024,128]{1,0:T(8,128)})) %all-reduce.31.cloned.1.call-update) | async-done | bytes 1048592 | tf_op jit(solution)/shard_map/psum | solution.py:44
  698.1 1.3 maximum_divide_fusion.2
  699.4 4.6 fusion.23
  704.0 2.4 fusion.45
  706.3 0.0 all-reduce.21.cloned.1.call-update
  706.4 0.3 all-reduce.29.cloned.1.call-start
  706.6 116.9 %all-reduce.21.cloned.1.call-done = (f32[128,896]{0,1:T(8,128)}, f32[128,896]{0,1:T(8,128)}) async-done(((f32[128,896]{0,1:T(8,128)}, f32[128,896]{0,1:T(8,128)}), (f32[128,896]{0,1:T(8,128)}, f32[128,896]{0,1:T(8,128)})) %all-reduce.21.cloned.1.call-update) | async-done | bytes 917520 | tf_op jit(solution)/shard_map/psum | solution.py:39
  823.6 1.2 maximum_divide_fusion.5
  824.8 4.0 fusion.18
  828.8 2.0 fusion.39
  830.7 0.0 all-reduce.29.cloned.1.call-update
  830.8 0.0 all-reduce.19.cloned.1.call-start
  830.8 92.2 %all-reduce.29.cloned.1.call-done = (f32[1024,128]{1,0:T(8,128)}, f32[1024,128]{1,0:T(8,128)}) async-done(((f32[1024,128]{1,0:T(8,128)}, f32[1024,128]{1,0:T(8,128)}), (f32[1024,128]{1,0:T(8,128)}, f32[1024,128]{1,0:T(8,128)})) %all-reduce.29.cloned.1.call-update) | async-done | bytes 1048592 | tf_op jit(solution)/shard_map/psum | solution.py:44
  923.0 1.3 maximum_divide_fusion.1
  924.3 4.6 fusion.22
  928.9 2.4 fusion.33
  931.3 0.0 all-reduce.27.cloned.1.call-start
  931.3 117.2 %all-reduce.19.cloned.1.call-done = (f32[128,896]{0,1:T(8,128)}, f32[128,896]{0,1:T(8,128)}) async-done(((f32[128,896]{0,1:T(8,128)}, f32[128,896]{0,1:T(8,128)}), (f32[128,896]{0,1:T(8,128)}, f32[128,896]{0,1:T(8,128)})) %all-reduce.19.cloned.1.call-update) | async-done | bytes 917520 | tf_op jit(solution)/shard_map/psum | solution.py:39
  1048.5 1.2 maximum_divide_fusion.4
  1049.7 4.0 fusion.17
  1053.7 2.0 fusion.30
  1055.7 1.0 copy.37
  1056.6 91.4 %all-reduce.27.cloned.1.call-done = (f32[1024,128]{1,0:T(8,128)}, f32[1024,128]{1,0:T(8,128)}) async-done(((f32[1024,128]{1,0:T(8,128)}, f32[1024,128]{1,0:T(8,128)}), (f32[1024,128]{1,0:T(8,128)}, f32[1024,128]{1,0:T(8,128)})) %all-reduce.27.cloned.1.call-update) | async-done | bytes 1048592 | tf_op jit(solution)/shard_map/psum | solution.py:44
  1148.0 2.1 maximum_divide_fusion
  (23 shorter events, 0.1 us)
Async XLA Ops:
  13.7 8.3 copy-start.2
  13.7 8.5 copy-start
  13.7 8.5 copy-start.3
  13.7 8.5 copy-start.4
  13.7 171.6 %all-to-all-start = ((bf16[8,1024,896]{2,1,0:T(8,128)(2,1)}), bf16[8,1024,896]{2,1,0:T(8,128)(2,1)}, u32[]{:S(2)}, u32[]{:S(2)}) async-start(bf16[8,1024,896]{2,1,0:T(8,128)(2,1)} %stack.2), calls=%async_computation | async-start | bytes 29360128 | tf_op jit(solution)/shard_map/all_to_all | solution.py:56
  21.9 351.8 %all-reduce.25.cloned.1.call-start = ((), (), s32[]{:S(2)}) async-start(), calls=%async_computation.4 | async-start | bytes 1835008 | tf_op jit(solution)/shard_map/psum | solution.py:39
  237.3 15.5 %copy-start.1 = (f32[128,896]{1,0:T(8,128)S(1)}, f32[128,896]{1,0:T(8,128)}, u32[]{:S(2)}) copy-start(f32[128,896]{1,0:T(8,128)} %param.11) | copy-start | bytes 1376260
  257.1 216.1 %all-reduce.33.cloned.1.call-start = ((), (), s32[]{:S(2)}) async-start(), calls=%async_computation.8 | async-start | bytes 2097152 | tf_op jit(solution)/shard_map/psum | solution.py:44
  380.9 217.7 %all-reduce.23.cloned.1.call-start = ((), (), s32[]{:S(2)}) async-start(), calls=%async_computation.3 | async-start | bytes 1835008 | tf_op jit(solution)/shard_map/psum | solution.py:39
  481.4 216.7 %all-reduce.31.cloned.1.call-start = ((), (), s32[]{:S(2)}) async-start(), calls=%async_computation.7 | async-start | bytes 2097152 | tf_op jit(solution)/shard_map/psum | solution.py:44
  605.8 217.8 %all-reduce.21.cloned.1.call-start = ((), (), s32[]{:S(2)}) async-start(), calls=%async_computation.2 | async-start | bytes 1835008 | tf_op jit(solution)/shard_map/psum | solution.py:39
  706.4 216.6 %all-reduce.29.cloned.1.call-start = ((), (), s32[]{:S(2)}) async-start(), calls=%async_computation.6 | async-start | bytes 2097152 | tf_op jit(solution)/shard_map/psum | solution.py:44
  830.8 217.7 %all-reduce.19.cloned.1.call-start = ((), (), s32[]{:S(2)}) async-start(), calls=%async_computation.1 | async-start | bytes 1835008 | tf_op jit(solution)/shard_map/psum | solution.py:39
  931.3 216.7 %all-reduce.27.cloned.1.call-start = ((), (), s32[]{:S(2)}) async-start(), calls=%async_computation.5 | async-start | bytes 2097152 | tf_op jit(solution)/shard_map/psum | solution.py:44
Sparse Core Ops, SparseCore 0:
  257.2 116.4 all-reduce.24
  381.0 92.0 all-reduce.32
  481.5 117.0 all-reduce.22
  605.9 92.1 all-reduce.30
  706.5 117.0 all-reduce.20
  830.9 92.0 all-reduce.28
  931.4 117.0 all-reduce.18
  1055.8 92.1 all-reduce.26
